TPU v7x, 32 devices: a whole 2x2x4 slice. The times are simulated.
32 devices in a mesh: segment: 2 (over y), fsdp: 4 (over x, core), seq: 4 (over z).
Axes of the slice: x: 2, y: 2, z: 4, core: 2. Of those that a mesh axis runs over, the one named last changes fastest.
Arguments:
- arriving: bfloat16 [2, 4, 768, 2048], P('segment', 'fsdp', 'seq'), may hold values from -6 to 6
- gain: float32 [2, 2048], P('segment'), may hold values from 0.1 to 1.9
- input_weight: bfloat16 [2, 2048, 16, 3, 128], P('segment', 'fsdp', 'seq')
- output_weight: bfloat16 [2, 16, 128, 2048], P('segment', 'seq', None, 'fsdp'), may hold values from -1 to 1
- block_pattern: int32 [2, 4, 24, 6], P('segment', 'fsdp'), may hold values from 0 to 23, as said below
Outputs:
- passed: bfloat16 [2, 4, 768, 2048], P('segment', 'fsdp', 'seq')
Inputs may be any that keep to these rules, and one draw needn't show every extreme that they name: `block_pattern`: row j of a document lists 6 different blocks; the first three are j - 1, j and j + 1 modulo 24, and block 0 is listed in every row.
All inputs are finite; a program needn't handle non-finite values.
Results may differ from a plain program's by a relative error of at most 0.012.
Values may be sent and summed in bfloat16 or wider, within the bound.
A program may use at most 64 MiB of HBM per device.

v0:
```python
import jax
import jax.numpy as jnp
from jax import lax
from jax.sharding import PartitionSpec as P

BLOCK = 32
SEL = 6
EPSILON = 1e-05


def passed_along(value, axis, steps):
    count = lax.axis_size(axis)
    pairs = [(source, (source + steps) % count) for source in range(count)]
    return lax.ppermute(value, axis, pairs)


def normalize(tokens, gain_row):
    values = tokens.astype(jnp.float32)
    spread = jnp.mean(values * values, axis=-1, keepdims=True)
    return (values * lax.rsqrt(spread + EPSILON) * gain_row).astype(jnp.bfloat16)


def attend(projected, pattern_rows):
    length, head_group, triple, head_width = projected.shape
    block_count = length // BLOCK
    query_rows = projected[:, :, 0].reshape(block_count, BLOCK, head_group, head_width)
    key_blocks = projected[:, :, 1].reshape(block_count, BLOCK, head_group, head_width)
    value_blocks = projected[:, :, 2].reshape(block_count, BLOCK, head_group, head_width)
    key_rows = jnp.take(key_blocks, pattern_rows, axis=0).reshape(
        block_count, SEL * BLOCK, head_group, head_width
    )
    value_rows = jnp.take(value_blocks, pattern_rows, axis=0).reshape(
        block_count, SEL * BLOCK, head_group, head_width
    )
    scores = jnp.einsum(
        "qbge,qnge->gqbn", query_rows, key_rows, preferred_element_type=jnp.float32
    ) * head_width ** (-0.5)
    row_max = jnp.max(scores, axis=-1, keepdims=True)
    exponent = jnp.exp(scores - row_max)
    weights = (exponent / jnp.sum(exponent, axis=-1, keepdims=True)).astype(jnp.bfloat16)
    mixed_rows = jnp.einsum(
        "gqbn,qnge->qbge", weights, value_rows, preferred_element_type=jnp.float32
    )
    return mixed_rows.astype(jnp.bfloat16).reshape(length, head_group * head_width)


def body(arriving, gain, input_weight, output_weight, block_pattern):
    tokens = arriving[0, 0]
    row_count = tokens.shape[0]
    normed = normalize(tokens, gain[0])
    slab_rows, head_group, triple, head_size = input_weight.shape[1:]
    columns = head_group * triple * head_size
    panel_flat = input_weight[0].reshape(slab_rows, columns)
    length = row_count * lax.axis_size("seq")
    whole_panel = lax.all_gather(panel_flat, "fsdp", axis=0, tiled=True)
    projected = jnp.dot(
        lax.all_gather(normed, "seq", axis=0, tiled=True),
        whole_panel,
        preferred_element_type=jnp.float32,
    )
    projected = projected.astype(jnp.bfloat16).reshape(length, head_group, triple, head_size)
    mixed_rows = attend(projected, block_pattern[0, 0])
    out_panel = output_weight[0].reshape(head_group * head_size, -1)
    whole_out = lax.all_gather(out_panel, "fsdp", axis=1, tiled=True)
    branch = lax.psum_scatter(
        jnp.dot(mixed_rows, whole_out, preferred_element_type=jnp.float32).astype(jnp.bfloat16),
        "seq",
        scatter_dimension=0,
        tiled=True,
    ).astype(jnp.float32)
    updated = (tokens.astype(jnp.float32) + branch).astype(jnp.bfloat16)
    passed = passed_along(updated, "segment", 1)
    return passed[None, None]


def solution(mesh):
    in_specs = (
        P("segment", "fsdp", "seq", None),
        P("segment", None),
        P("segment", "fsdp", "seq", None, None),
        P("segment", "seq", None, "fsdp"),
        P("segment", "fsdp", None, None),
    )
    out_specs = P("segment", "fsdp", "seq", None)
    return jax.shard_map(body, mesh=mesh, in_specs=in_specs, out_specs=out_specs, check_vma=False)
```

profile of v0, /device:TPU:0, one launch (start us, length us, event | category | flops | bytes accessed | tf_op | source)
XLA Modules:
  0.0 277.0 jit_solution(2608817675597869169)
XLA Ops:
  6.5 0.0 copy-start.1
  6.5 0.0 all-gather.4.cloned.1.call-start
  6.5 1.5 fusion.4
  8.0 2.3 fusion.6
  10.3 0.0 copy-start.2
  10.3 0.0 all-gather.4.cloned.1.call-update
  10.3 0.0 all-gather.6.cloned.1.call-start
  10.4 0.0 copy-done.1
  10.4 2.6 copy.24
  13.0 0.0 all-gather.6.cloned.1.call-update
  13.0 0.0 all-gather.8.cloned.1.call-start
  13.0 0.7 all-gather.8.cloned.1.call-update
  13.7 0.0 reduce-scatter.2.cloned.1.call-start
  13.8 0.0 copy-done.2
  13.8 0.1 copy.27
  13.9 0.1 reshape.54
  14.0 0.1 copy.23
  14.1 62.6 %all-gather.4.cloned.1.call-done = bf16[768,2048]{1,0:T(8,128)(2,1)} async-done(((bf16[192,2048]{1,0:T(8,128)(2,1)}), bf16[768,2048]{1,0:T(8,128)(2,1)}) %all-gather.4.cloned.1.call-update) | async-done | bytes 3145744 | tf_op jit(solution)/shard_map/all_gather | solution.py:57
  76.7 46.6 %all-gather.6.cloned.1.call-done = bf16[2048,1536]{0,1:T(8,128)(2,1)} async-done(((bf16[512,1536]{0,1:T(8,128)(2,1)}), bf16[2048,1536]{0,1:T(8,128)(2,1)}) %all-gather.6.cloned.1.call-update) | async-done | bytes 6291472 | tf_op jit(solution)/shard_map/all_gather | solution.py:55
  123.3 9.3 %convolution_convert_fusion.1 = bf16[768,1536]{1,0:T(8,128)(2,1)} fusion(bf16[768,2048]{1,0:T(8,128)(2,1)} %all-gather.4.cloned.1.call-done, bf16[2048,1536]{0,1:T(8,128)(2,1)} %all-gather.6.cloned.1.call-done), kind=kOutput, calls=%fused_computation.6 | convolution fusion | flops 4833017856 | bytes 11796480 | tf_op jit(solution)/shard_map/dot_general | solution.py:56
  132.6 2.9 %copy.25 = bf16[768,1536]{0,1:T(8,128)(2,1)S(1)} copy(bf16[768,1536]{1,0:T(8,128)(2,1)} %convolution_convert_fusion.1) | data formatting | bytes 4718592 | tf_op jit(solution)/shard_map/convert_element_type | solution.py:61
  135.5 1.3 fusion.20
  136.8 1.5 copy.31
  138.3 1.5 copy.26
  139.8 7.6 %gather_fusion.1 = bf16[144,32,4,128]{3,1,2,0:T(8,128)(2,1)} fusion(bf16[24,32,4,128]{3,1,0,2:T(8,128)(2,1)S(1)} %bitcast.37, s32[1024]{0:T(1024)S(1)} %pad_clamp_fusion), kind=kCustom, calls=%fused_computation.1.clone | custom fusion | bytes 9437760 | tf_op jit(solution)/shard_map/jit(_take)/gather | solution.py:29
  147.4 7.6 %gather_fusion = bf16[144,32,4,128]{3,1,2,0:T(8,128)(2,1)} fusion(bf16[24,32,4,128]{3,1,0,2:T(8,128)(2,1)S(1)} %bitcast.36, s32[1024]{0:T(1024)S(1)} %pad_clamp_fusion), kind=kCustom, calls=%fused_computation.clone | custom fusion | bytes 9437760 | tf_op jit(solution)/shard_map/jit(_take)/gather | solution.py:32
  155.0 5.7 %broadcast_select_fusion = (bf16[24,6,32,4,128]{4,2,3,1,0:T(8,128)(2,1)S(1)}, bf16[24,6,32,4,128]{4,2,3,1,0:T(8,128)(2,1)}) fusion(bf16[24,6,32,4,128]{4,2,3,1,0:T(8,128)(2,1)} %bitcast.38, pred[24,6]{1,0:T(8,128)(4,1)S(1)} %copy.23, bf16[24,6,32,4,128]{4,2,3,1,0:T(8,128)(2,1)} %bitcast.39), kind=kLoop, calls=%fused_computation.3 | loop fusion | flops 4718592 | bytes 18874512 | tf_op jit(solution)/shard_map/jit(_take)/select_n | solution.py:29
  160.7 3.6 %copy.33 = bf16[24,6,32,4,128]{4,2,1,0,3:T(8,128)(2,1)} copy(bf16[24,6,32,4,128]{4,2,3,1,0:T(8,128)(2,1)S(1)} %get-tuple-element.9) | data formatting | bytes 9437184 | tf_op jit(solution)/shard_map/jit(_take)/select_n | solution.py:29
  164.2 0.4 copy.29
  164.6 5.9 %copy.28 = bf16[24,6,32,4,128]{4,2,1,3,0:T(8,128)(2,1)} copy(bf16[24,6,32,4,128]{4,2,3,1,0:T(8,128)(2,1)} %get-tuple-element.10) | data formatting | bytes 9437184 | tf_op jit(solution)/shard_map/jit(_take)/select_n | solution.py:32
  170.5 7.2 %fusion.21 = (f32[4,24,32]{2,1,0:T(8,128)S(1)}, f32[4,24,32,192]{3,2,1,0:T(8,128)}) fusion(bf16[24,32,4,128]{3,1,0,2:T(8,128)(2,1)S(1)} %bitcast.44, bf16[24,192,4,128]{3,1,0,2:T(8,128)(2,1)} %bitcast.40), kind=kOutput, calls=%fused_computation.31 | convolution fusion | flops 152764608 | bytes 7876608 | tf_op jit(solution)/shard_map/sub | solution.py:39
  177.7 5.2 %fusion.14 = bf16[24,32,4,128]{3,1,2,0:T(8,128)(2,1)S(1)} fusion(bf16[24,192,4,128]{3,1,2,0:T(8,128)(2,1)} %bitcast.43, f32[4,24,32,192]{3,2,1,0:T(8,128)} %get-tuple-element.12, f32[4,24,32]{2,1,0:T(8,128)S(1)} %get-tuple-element.11), kind=kOutput, calls=%fused_computation.22 | convolution fusion | flops 152567808 | bytes 7876608 | tf_op jit(solution)/shard_map/gqbn,qnge->qbge/dot_general | solution.py:41
  182.9 0.4 copy.35
  183.3 0.0 all-gather.8.cloned.1.call-done
  183.3 5.0 %convolution_convert_fusion = bf16[768,2048]{1,0:T(8,128)(2,1)} fusion(bf16[512,2048]{1,0:T(8,128)(2,1)} %all-gather.8.cloned.1.call-done, bf16[96,8,4,128]{3,2,1,0:T(4,128)(2,1)S(1)} %bitcast.45), kind=kOutput, calls=%fused_computation.5 | convolution fusion | flops 1612185600 | bytes 6029312 | tf_op jit(solution)/shard_map/dot_general | solution.py:66
  188.3 0.0 copy-start
  188.3 0.0 reduce-scatter.2.cloned.1.call-update
  188.4 60.6 %reduce-scatter.2.cloned.1.call-done = bf16[192,2048]{1,0:T(8,128)(2,1)} async-done(((bf16[768,2048]{1,0:T(8,128)(2,1)}), bf16[192,2048]{1,0:T(8,128)(2,1)}) %reduce-scatter.2.cloned.1.call-update) | async-done | bytes 786448 | tf_op jit(solution)/shard_map/reduce_scatter | solution.py:65
  248.9 0.0 copy-done
  248.9 1.4 fusion.7
  250.4 1.5 collective-permute-start
  251.9 17.7 %collective-permute-done = bf16[192,2048]{1,0:T(8,128)(2,1)S(1)} collective-permute-done((bf16[192,2048]{1,0:T(8,128)(2,1)S(1)}, bf16[192,2048]{1,0:T(8,128)(2,1)S(1)}, u32[]{:S(2)}, u32[]{:S(2)}) %collective-permute-start) | collective-permute-done | bytes 786464 | tf_op jit(solution)/shard_map/ppermute | solution.py:14
  269.5 0.9 copy.52
  (4 shorter events, 0.0 us)
Async XLA Ops:
  6.5 3.8 %copy-start.1 = (bf16[1,512,4,3,128]{4,2,3,1,0:T(4,128)(2,1)S(1)}, bf16[1,512,4,3,128]{4,2,3,1,0:T(4,128)(2,1)}, u32[]{:S(2)}) copy-start(bf16[1,512,4,3,128]{4,2,3,1,0:T(4,128)(2,1)} %param.9) | copy-start | bytes 4718596
  6.5 70.1 %all-gather.4.cloned.1.call-start = ((), (), s32[]{:S(2)}) async-start(), calls=%async_computation.1 | async-start | bytes 3932160 | tf_op jit(solution)/shard_map/all_gather | solution.py:57
  10.3 3.5 %copy-start.2 = (s32[1,1,24,6]{2,1,3,0:T(1,128)S(1)}, s32[1,1,24,6]{2,1,3,0:T(1,128)}, u32[]{:S(2)}) copy-start(s32[1,1,24,6]{2,1,3,0:T(1,128)} %param.11) | copy-start | bytes 1732
  10.3 113.0 %all-gather.6.cloned.1.call-start = ((), (), s32[]{:S(2)}) async-start(), calls=%async_computation.2 | async-start | bytes 7864320 | tf_op jit(solution)/shard_map/all_gather | solution.py:55
  13.0 170.3 %all-gather.8.cloned.1.call-start = ((), (), s32[]{:S(2)}) async-start(), calls=%async_computation.3 | async-start | bytes 2621440 | tf_op jit(solution)/shard_map/all_gather | solution.py:64
  13.7 235.2 %reduce-scatter.2.cloned.1.call-start = ((), (), s32[]{:S(2)}) async-start(), calls=%async_computation.4 | async-start | bytes 3932160 | tf_op jit(solution)/shard_map/reduce_scatter | solution.py:65
  188.3 60.6 %copy-start = (bf16[1,1,192,2048]{3,2,1,0:T(8,128)(2,1)S(1)}, bf16[1,1,192,2048]{3,2,1,0:T(8,128)(2,1)}, u32[]{:S(2)}) copy-start(bf16[1,1,192,2048]{3,2,1,0:T(8,128)(2,1)} %param.7) | copy-start | bytes 2359300
  250.4 19.2 %collective-permute-start = (bf16[192,2048]{1,0:T(8,128)(2,1)S(1)}, bf16[192,2048]{1,0:T(8,128)(2,1)S(1)}, u32[]{:S(2)}, u32[]{:S(2)}) collective-permute-start(bf16[192,2048]{1,0:T(8,128)(2,1)S(1)} %fusion.7), channel_id=1, source_target_pairs={{0,16},{16,0},{1,17},{17,1},{2,18},{18,2},{3,19},{19,3},{4,20},{20... | collective-permute-start | bytes 2359304 | tf_op jit(solution)/shard_map/ppermute | solution.py:14
Sparse Core Ops, SparseCore 0:
  10.5 66.1 all-gather.3
  78.2 45.0 all-gather.5
  124.9 22.5 all-gather.7
  188.5 60.4 reduce-scatter.1
where the time goes:
time: 277 us
  waiting for transfers between devices  188 us (68%)
  local copies, waits for them, and re-layouts  36.4 us (13%)
  matrix products  26.7 us (10%)
  between operations  13.2 us (5%)
  other arithmetic  10.8 us (4%)
    all_gather x1, waiting for transfers between devices, body(): lax.all_gather(normed, 'seq', axis=0, tiled=True)  62.6 us
    reduce_scatter x1, waiting for transfers between devices, body(): lax.psum_scatter(jnp.dot(mixed_rows, whole_out, preferred_element_type=jn...  60.6 us
    all_gather x1, waiting for transfers between devices, body(): whole_panel = lax.all_gather(panel_flat, 'fsdp', axis=0, tiled=True)  46.6 us
    ppermute x1, waiting for transfers between devices, passed_along(): return lax.ppermute(value, axis, pairs)  17.7 us
    dot_general x1, matrix products, body(): jnp.dot(lax.all_gather(normed, 'seq', axis=0, tiled=True), whole_panel, p...  9.27 us
    gather x1, local copies, waits for them, and re-layouts, attend(): jnp.take(value_blocks, pattern_rows, axis=0)  7.62 us
    gather x1, local copies, waits for them, and re-layouts, attend(): jnp.take(key_blocks, pattern_rows, axis=0)  7.56 us
    sub x1, matrix products, attend(): exponent = jnp.exp(scores - row_max)  7.16 us
  transfers between devices with their start and end apart: 5, of which 4 were waited for; matrix products, arithmetic and copies ran while one was open for 23% of the time, Pallas kernels for 0%

commit v1 on v0

--- a/solution.py
+++ b/solution.py
@@ -52,7 +52,12 @@
     columns = head_group * triple * head_size
     panel_flat = input_weight[0].reshape(slab_rows, columns)
     length = row_count * lax.axis_size("seq")
-    whole_panel = lax.all_gather(panel_flat, "fsdp", axis=0, tiled=True)
+    ring = [panel_flat]
+    for hop in range(3):
+        ring.append(lax.ppermute(ring[-1], "fsdp", [(dev, (dev + 1) % 4) for dev in range(4)]))
+    whole_panel = jnp.roll(
+        jnp.concatenate(ring[::-1], axis=0), (lax.axis_index("fsdp") + 1) * ring[0].shape[0], axis=0
+    )
     projected = jnp.dot(
         lax.all_gather(normed, "seq", axis=0, tiled=True),
         whole_panel,

time: 277 us -> 245 us (0.88)
  waiting for transfers between devices: 188 us -> 140 us
  local copies, waits for them, and re-layouts: 36.4 us -> 51.4 us
    all_gather x1, waiting for transfers between devices: 62.6 us -> 0.01 us  [body(): lax.all_gather(normed, 'seq', axis=0, tiled=True)]
    ppermute x0 -> x3, waiting for transfers between devices: none -> 59.7 us  [body(): lax.ppermute(ring[-1], 'fsdp', [(dev, (dev + 1) % 4) for dev in range(4)])]
    all_gather x1 -> x0, waiting for transfers between devices: 46.6 us -> none  [body(): whole_panel = lax.all_gather(panel_flat, 'fsdp', axis=0, tiled=True)]
    unnamed x8 -> x15, local copies, waits for them, and re-layouts: 3.47 us -> 17.3 us
  transfers between devices with their start and end apart: 5 -> 7, of which waited for: 4 -> 5; matrix products, arithmetic and copies ran while one was open for 23% -> 32% of each run, Pallas kernels for 0% -> 0%
where the time goes in v1:
time: 245 us
  waiting for transfers between devices  140 us (57%)
  local copies, waits for them, and re-layouts  51.4 us (21%)
  matrix products  26.8 us (11%)
  between operations  13.2 us (5%)
  other arithmetic  10.9 us (4%)
    reduce_scatter x1, waiting for transfers between devices, body(): lax.psum_scatter(jnp.dot(mixed_rows, whole_out, preferred_element_type=jn...  62.7 us
    ppermute x3, waiting for transfers between devices, body(): lax.ppermute(ring[-1], 'fsdp', [(dev, (dev + 1) % 4) for dev in range(4)])  59.7 us
    ppermute x1, waiting for transfers between devices, passed_along(): return lax.ppermute(value, axis, pairs)  17.6 us
    unnamed x15, local copies, waits for them, and re-layouts  17.3 us
    dot_general x1, matrix products, body(): jnp.dot(lax.all_gather(normed, 'seq', axis=0, tiled=True), whole_panel, p...  9.33 us
    gather x1, local copies, waits for them, and re-layouts, attend(): jnp.take(key_blocks, pattern_rows, axis=0)  7.63 us
    gather x1, local copies, waits for them, and re-layouts, attend(): jnp.take(value_blocks, pattern_rows, axis=0)  7.52 us
    sub x1, matrix products, attend(): exponent = jnp.exp(scores - row_max)  7.18 us
  transfers between devices with their start and end apart: 7, of which 5 were waited for; matrix products, arithmetic and copies ran while one was open for 32% of the time, Pallas kernels for 0%

profile of v1, /device:TPU:0, one launch (start us, length us, event | category | flops | bytes accessed | tf_op | source)
XLA Modules:
  0.0 244.5 jit_solution(12368732960169958544)
XLA Ops:
  6.5 0.0 all-gather.3.cloned.1.call-start
  6.5 1.5 fusion.9
  8.0 2.3 fusion.11
  10.3 0.0 all-gather.3.cloned.1.call-update
  10.3 0.0 all-gather.5.cloned.1.call-start
  10.4 1.4 copy.24
  11.8 0.5 collective-permute-start
  12.3 20.0 %collective-permute-done = bf16[512,1536]{0,1:T(8,128)(2,1)S(1)} collective-permute-done((bf16[512,1536]{0,1:T(8,128)(2,1)S(1)}, bf16[512,1536]{0,1:T(8,128)(2,1)S(1)}, u32[]{:S(2)}, u32[]{:S(2)}) %collective-permute-start) | collective-permute-done | bytes 1572896 | tf_op jit(solution)/shard_map/ppermute | solution.py:57
  32.4 0.0 collective-permute-start.1
  32.4 19.9 %collective-permute-done.1 = bf16[512,1536]{0,1:T(8,128)(2,1)} collective-permute-done((bf16[512,1536]{0,1:T(8,128)(2,1)S(1)}, bf16[512,1536]{0,1:T(8,128)(2,1)}, u32[]{:S(2)}, u32[]{:S(2)}) %collective-permute-start.1) | collective-permute-done | bytes 1572896 | tf_op jit(solution)/shard_map/ppermute | solution.py:57
  52.3 0.0 collective-permute-start.2
  52.3 0.0 all-gather.5.cloned.1.call-update
  52.3 0.0 reduce-scatter.2.cloned.1.call-start
  52.4 0.0 copy-done.2
  52.4 0.1 copy.27
  52.5 0.1 reshape.54
  52.6 0.1 copy.23
  52.7 19.7 %collective-permute-done.2 = bf16[512,1536]{0,1:T(8,128)(2,1)} collective-permute-done((bf16[512,1536]{0,1:T(8,128)(2,1)}, bf16[512,1536]{0,1:T(8,128)(2,1)}, u32[]{:S(2)}, u32[]{:S(2)}) %collective-permute-start.2) | collective-permute-done | bytes 1572896 | tf_op jit(solution)/shard_map/ppermute | solution.py:57
  72.5 2.8 %constant_dynamic-update-slice_fusion.7 = bf16[4096,1536]{0,1:T(8,128)(2,1)} fusion(bf16[512,1536]{0,1:T(8,128)(2,1)} %collective-permute-done.2), kind=kLoop, calls=%fused_computation.34 | loop fusion | bytes 3145728
  75.2 2.8 %constant_dynamic-update-slice_fusion.6 = bf16[4096,1536]{0,1:T(8,128)(2,1)} fusion(bf16[4096,1536]{0,1:T(8,128)(2,1)} %constant_dynamic-update-slice_fusion.7, bf16[512,1536]{0,1:T(8,128)(2,1)} %collective-permute-done.1), kind=kLoop, calls=%fused_computation.33 | loop fusion | bytes 3145728
  78.0 1.3 constant_dynamic-update-slice_fusion.5
  79.3 1.3 constant_dynamic-update-slice_fusion.4
  80.7 2.7 %constant_dynamic-update-slice_fusion.3 = bf16[4096,1536]{0,1:T(8,128)(2,1)} fusion(bf16[4096,1536]{0,1:T(8,128)(2,1)} %constant_dynamic-update-slice_fusion.4, bf16[512,1536]{0,1:T(8,128)(2,1)} %collective-permute-done.2), kind=kLoop, calls=%fused_computation.30 | loop fusion | bytes 3145728
  83.4 2.8 %constant_dynamic-update-slice_fusion.2 = bf16[4096,1536]{0,1:T(8,128)(2,1)} fusion(bf16[4096,1536]{0,1:T(8,128)(2,1)} %constant_dynamic-update-slice_fusion.3, bf16[512,1536]{0,1:T(8,128)(2,1)} %collective-permute-done.1), kind=kLoop, calls=%fused_computation.29 | loop fusion | bytes 3145728
  86.1 1.3 constant_dynamic-update-slice_fusion.1
  87.5 1.3 constant_dynamic-update-slice_fusion
  88.8 9.3 %fusion.3 = bf16[768,1536]{1,0:T(8,128)(2,1)} fusion(bf16[768,2048]{1,0:T(8,128)(2,1)} %all-gather.3.cloned.1.call-done, bf16[4096,1536]{0,1:T(8,128)(2,1)} %constant_dynamic-update-slice_fusion, s32[]{:T(128)S(6)} %select_n.21), kind=kOutput, calls=%fused_computation.7 | convolution fusion | flops 4833017856 | bytes 11796484 | tf_op jit(solution)/shard_map/dot_general | solution.py:61
  98.1 2.8 %copy.25 = bf16[768,1536]{0,1:T(8,128)(2,1)S(1)} copy(bf16[768,1536]{1,0:T(8,128)(2,1)} %fusion.3) | data formatting | bytes 4718592 | tf_op jit(solution)/shard_map/convert_element_type | solution.py:66
  100.9 1.3 fusion.26
  102.2 1.5 copy.31
  103.7 1.5 copy.26
  105.2 7.6 %gather_fusion.1 = bf16[144,32,4,128]{3,1,2,0:T(8,128)(2,1)} fusion(bf16[24,32,4,128]{3,1,0,2:T(8,128)(2,1)S(1)} %bitcast.36, s32[1024]{0:T(1024)S(1)} %pad_clamp_fusion), kind=kCustom, calls=%fused_computation.1.clone | custom fusion | bytes 9437760 | tf_op jit(solution)/shard_map/jit(_take)/gather | solution.py:29
  112.9 7.5 %gather_fusion = bf16[144,32,4,128]{3,1,2,0:T(8,128)(2,1)} fusion(bf16[24,32,4,128]{3,1,0,2:T(8,128)(2,1)S(1)} %bitcast.35, s32[1024]{0:T(1024)S(1)} %pad_clamp_fusion), kind=kCustom, calls=%fused_computation.clone | custom fusion | bytes 9437760 | tf_op jit(solution)/shard_map/jit(_take)/gather | solution.py:32
  120.4 5.7 %broadcast_select_fusion = (bf16[24,6,32,4,128]{4,2,3,1,0:T(8,128)(2,1)S(1)}, bf16[24,6,32,4,128]{4,2,3,1,0:T(8,128)(2,1)}) fusion(bf16[24,6,32,4,128]{4,2,3,1,0:T(8,128)(2,1)} %bitcast.37, pred[24,6]{1,0:T(8,128)(4,1)S(1)} %copy.23, bf16[24,6,32,4,128]{4,2,3,1,0:T(8,128)(2,1)} %bitcast.38), kind=kLoop, calls=%fused_computation.5 | loop fusion | flops 4718592 | bytes 18874512 | tf_op jit(solution)/shard_map/jit(_take)/select_n | solution.py:29
  126.1 3.5 %copy.33 = bf16[24,6,32,4,128]{4,2,1,0,3:T(8,128)(2,1)} copy(bf16[24,6,32,4,128]{4,2,3,1,0:T(8,128)(2,1)S(1)} %get-tuple-element.9) | data formatting | bytes 9437184 | tf_op jit(solution)/shard_map/jit(_take)/select_n | solution.py:29
  129.6 0.4 copy.29
  130.0 6.0 %copy.28 = bf16[24,6,32,4,128]{4,2,1,3,0:T(8,128)(2,1)} copy(bf16[24,6,32,4,128]{4,2,3,1,0:T(8,128)(2,1)} %get-tuple-element.10) | data formatting | bytes 9437184 | tf_op jit(solution)/shard_map/jit(_take)/select_n | solution.py:32
  135.9 7.2 %fusion.27 = (f32[4,24,32]{2,1,0:T(8,128)S(1)}, f32[4,24,32,192]{3,2,1,0:T(8,128)}) fusion(bf16[24,32,4,128]{3,1,0,2:T(8,128)(2,1)S(1)} %bitcast.45, bf16[24,192,4,128]{3,1,0,2:T(8,128)(2,1)} %bitcast.39), kind=kOutput, calls=%fused_computation.42 | convolution fusion | flops 152764608 | bytes 7876608 | tf_op jit(solution)/shard_map/sub | solution.py:39
  143.1 5.2 %fusion.19 = bf16[24,32,4,128]{3,1,2,0:T(8,128)(2,1)S(1)} fusion(bf16[24,192,4,128]{3,1,2,0:T(8,128)(2,1)} %bitcast.44, f32[4,24,32,192]{3,2,1,0:T(8,128)} %get-tuple-element.12, f32[4,24,32]{2,1,0:T(8,128)S(1)} %get-tuple-element.11), kind=kOutput, calls=%fused_computation.24 | convolution fusion | flops 152567808 | bytes 7876608 | tf_op jit(solution)/shard_map/gqbn,qnge->qbge/dot_general | solution.py:41
  148.3 0.4 copy.35
  148.7 0.0 all-gather.5.cloned.1.call-done
  148.8 5.1 %convolution_convert_fusion = bf16[768,2048]{1,0:T(8,128)(2,1)} fusion(bf16[512,2048]{1,0:T(8,128)(2,1)} %all-gather.5.cloned.1.call-done, bf16[96,8,4,128]{3,2,1,0:T(4,128)(2,1)S(1)} %bitcast.46), kind=kOutput, calls=%fused_computation.8 | convolution fusion | flops 1612185600 | bytes 6029312 | tf_op jit(solution)/shard_map/dot_general | solution.py:71
  153.8 0.0 reduce-scatter.2.cloned.1.call-update
  153.9 62.7 %reduce-scatter.2.cloned.1.call-done = bf16[192,2048]{1,0:T(8,128)(2,1)} async-done(((bf16[768,2048]{1,0:T(8,128)(2,1)}), bf16[192,2048]{1,0:T(8,128)(2,1)}) %reduce-scatter.2.cloned.1.call-update) | async-done | bytes 786448 | tf_op jit(solution)/shard_map/reduce_scatter | solution.py:70
  216.6 1.4 fusion.12
  218.0 1.5 collective-permute-start.3
  219.5 17.6 %collective-permute-done.3 = bf16[192,2048]{1,0:T(8,128)(2,1)S(1)} collective-permute-done((bf16[192,2048]{1,0:T(8,128)(2,1)S(1)}, bf16[192,2048]{1,0:T(8,128)(2,1)S(1)}, u32[]{:S(2)}, u32[]{:S(2)}) %collective-permute-start.3) | collective-permute-done | bytes 786464 | tf_op jit(solution)/shard_map/ppermute | solution.py:14
  237.1 0.9 copy.59
  (10 shorter events, 0.0 us)
Async XLA Ops:
  6.5 3.8 %copy-start.1 = (bf16[1,512,4,3,128]{4,2,3,1,0:T(4,128)(2,1)S(1)}, bf16[1,512,4,3,128]{4,2,3,1,0:T(4,128)(2,1)}, u32[]{:S(2)}) copy-start(bf16[1,512,4,3,128]{4,2,3,1,0:T(4,128)(2,1)} %param.9) | copy-start | bytes 4718596
  6.5 82.2 %all-gather.3.cloned.1.call-start = ((), (), s32[]{:S(2)}) async-start(), calls=%async_computation.1 | async-start | bytes 3932160 | tf_op jit(solution)/shard_map/all_gather | solution.py:62
  8.0 44.4 %copy-start.2 = (s32[1,1,24,6]{2,1,3,0:T(1,128)S(1)}, s32[1,1,24,6]{2,1,3,0:T(1,128)}, u32[]{:S(2)}) copy-start(s32[1,1,24,6]{2,1,3,0:T(1,128)} %param.11) | copy-start | bytes 1732
  10.3 138.4 %all-gather.5.cloned.1.call-start = ((), (), s32[]{:S(2)}) async-start(), calls=%async_computation.2 | async-start | bytes 2621440 | tf_op jit(solution)/shard_map/all_gather | solution.py:69
  11.8 20.5 %collective-permute-start = (bf16[512,1536]{0,1:T(8,128)(2,1)S(1)}, bf16[512,1536]{0,1:T(8,128)(2,1)S(1)}, u32[]{:S(2)}, u32[]{:S(2)}) collective-permute-start(bf16[512,1536]{0,1:T(8,128)(2,1)S(1)} %bitcast.40), channel_id=1, source_target_pairs={{0,4},{4,8},{8,12},{12,0},{1,5},{5,9},{9,13},{13,1},{2,6},{6,10},{... | collective-permute-start | bytes 4718600 | tf_op jit(solution)/shard_map/ppermute | solution.py:57
  32.4 19.9 %collective-permute-start.1 = (bf16[512,1536]{0,1:T(8,128)(2,1)S(1)}, bf16[512,1536]{0,1:T(8,128)(2,1)}, u32[]{:S(2)}, u32[]{:S(2)}) collective-permute-start(bf16[512,1536]{0,1:T(8,128)(2,1)S(1)} %collective-permute-done), channel_id=1, source_target_pairs={{0,4},{4,8},{8,12},{12,0},{1,5},{5,9},{9,13},{13,1},{2,6},{6,10},{... | collective-permute-start | bytes 4718600 | tf_op jit(solution)/shard_map/ppermute | solution.py:57
  52.3 20.2 %collective-permute-start.2 = (bf16[512,1536]{0,1:T(8,128)(2,1)}, bf16[512,1536]{0,1:T(8,128)(2,1)}, u32[]{:S(2)}, u32[]{:S(2)}) collective-permute-start(bf16[512,1536]{0,1:T(8,128)(2,1)} %collective-permute-done.1), channel_id=1, source_target_pairs={{0,4},{4,8},{8,12},{12,0},{1,5},{5,9},{9,13},{13,1},{2,6},{6,10},{... | collective-permute-start | bytes 4718600 | tf_op jit(solution)/shard_map/ppermute | solution.py:57
  52.3 164.2 %reduce-scatter.2.cloned.1.call-start = ((), (), s32[]{:S(2)}) async-start(), calls=%async_computation.3 | async-start | bytes 3932160 | tf_op jit(solution)/shard_map/reduce_scatter | solution.py:70
  153.8 62.7 %copy-start = (bf16[1,1,192,2048]{3,2,1,0:T(8,128)(2,1)S(1)}, bf16[1,1,192,2048]{3,2,1,0:T(8,128)(2,1)}, u32[]{:S(2)}) copy-start(bf16[1,1,192,2048]{3,2,1,0:T(8,128)(2,1)} %param.7) | copy-start | bytes 2359300
  218.0 19.2 %collective-permute-start.3 = (bf16[192,2048]{1,0:T(8,128)(2,1)S(1)}, bf16[192,2048]{1,0:T(8,128)(2,1)S(1)}, u32[]{:S(2)}, u32[]{:S(2)}) collective-permute-start(bf16[192,2048]{1,0:T(8,128)(2,1)S(1)} %fusion.12), channel_id=1, source_target_pairs={{0,16},{16,0},{1,17},{17,1},{2,18},{18,2},{3,19},{19,3},{4,20},{20... | collective-permute-start | bytes 2359304 | tf_op jit(solution)/shard_map/ppermute | solution.py:14
Sparse Core Ops, SparseCore 0:
  10.5 66.1 all-gather.2
  78.2 21.2 all-gather.4
  154.0 62.5 reduce-scatter.1
